TPU v7x, 256 devices: a whole 4x4x8 slice. The times are simulated.
256 devices in a mesh: lsec: 16 (over x, z_lo), rsec: 16 (over z_hi, y, core).
Axes of the slice: x: 4, y: 4, z: 8 (z_hi: 2, z_lo: 4; z = z_hi * 4 + z_lo), core: 2. Of those that a mesh axis runs over, the one named last changes fastest.
Arguments:
- states: float32 [2, 10240, 10240], P(None, 'lsec', 'rsec'), may hold values from -6 to 6
- left_env: float32 [16, 640, 640], P('lsec', 'rsec'), may hold values from -0.25 to 0.25
- right_env: float32 [16, 640, 640], P('rsec', 'lsec'), may hold values from -0.25 to 0.25
- left_op: float32 [16, 640, 640], P('lsec', 'rsec'), may hold values from -0.25 to 0.25
- right_op: float32 [16, 640, 640], P('rsec', 'lsec'), may hold values from -0.25 to 0.25
- sizes_left: int32 [16], P('lsec'), may hold values from 320 to 640
- sizes_right: int32 [16], P('rsec'), may hold values from 320 to 640
Outputs:
- applied: float32 [2, 10240, 10240], P(None, 'lsec', 'rsec')
All inputs are finite; a program needn't handle non-finite values.
Results may differ from a plain program's by a relative error of at most 0.000059.
Values sent between devices are 32-bit elements; how exact they have to be, the bound alone decides.
A program may use at most 128 MiB of HBM per device.

v0:
```python
import jax
import jax.numpy as jnp
from jax import lax
from jax.sharding import PartitionSpec as P

HI = lax.Precision.HIGH


def shifted(value, step):
    n, m = (lax.axis_size("lsec"), lax.axis_size("rsec"))
    pairs = [
        (i * m + j, (i + step) * m + j - step)
        for i in range(n)
        for j in range(m)
        if 0 <= i + step < n and 0 <= j - step < m
    ]
    return lax.ppermute(value, ("lsec", "rsec"), pairs)


def on_device(states, left_env, right_env, left_op, right_op, sizes_left, sizes_right):
    width = states.shape[1]
    rows = jnp.arange(width, dtype=jnp.int32)
    mask = (rows[:, None] < sizes_left[0]).astype(jnp.float32) * (
        rows[None, :] < sizes_right[0]
    ).astype(jnp.float32)
    masked = states * mask[None]
    moved = shifted(masked, 1)
    left = lax.all_gather(jnp.concatenate([left_env, left_op]), "rsec", axis=1, tiled=True)
    right = lax.all_gather(jnp.concatenate([right_env, right_op]), "lsec", axis=1, tiled=True)
    env_l, oper_l, env_r, oper_r = (left[0], left[1], right[0], right[1])
    right_part = jnp.einsum("rbc,cd->rbd", masked, oper_r, precision=HI)
    source = jnp.einsum("ba,rbd->rad", oper_l, right_part, precision=HI)
    back = shifted(source, -1)
    local = jnp.einsum("ab,rbc->rac", env_l, masked, precision=HI)
    local = local + jnp.einsum("rbc,dc->rbd", masked, env_r, precision=HI)
    inner = jnp.einsum("rbc,dc->rbd", moved, oper_r, precision=HI)
    hop = jnp.einsum("ab,rbd->rad", oper_l, inner, precision=HI)
    return (local + hop + back) * mask[None]


def solution(mesh):
    in_specs = (
        P(None, "lsec", "rsec"),
        P("lsec", "rsec", None),
        P("rsec", "lsec", None),
        P("lsec", "rsec", None),
        P("rsec", "lsec", None),
        P("lsec"),
        P("rsec"),
    )
    out_specs = P(None, "lsec", "rsec")
    return jax.shard_map(
        on_device, mesh=mesh, in_specs=in_specs, out_specs=out_specs, check_vma=False
    )
```

profile of v0, /device:TPU:198, one launch (start us, length us, event | category | flops | bytes accessed | tf_op | source)
XLA Modules:
  0.0 410.6 jit_solution(3178163259722050696)
XLA Ops:
  6.5 0.0 all-gather.5.cloned.1.call-start
  6.5 1.6 pad_maximum_fusion.1
  8.2 0.0 all-gather.5.cloned.1.call-update
  8.2 0.0 all-gather.3.cloned.1.call-start
  8.2 1.7 pad_maximum_fusion
  9.9 0.0 all-gather.3.cloned.1.call-update
  11.2 4.6 %copy.8 = f32[2,640,640]{1,2,0:T(8,128)} copy(f32[2,640,640]{2,1,0:T(8,128)} %param.7) | data formatting | bytes 6553600 | tf_op args[0]
  15.8 0.2 broadcast_multiply_fusion.1
  16.0 0.0 copy-start
  16.0 2.8 broadcast_multiply_fusion
  18.8 0.0 copy-done
  18.8 4.8 %collective-permute-start = (f32[2,640,640]{1,2,0:T(8,128)S(1)}, f32[2,640,640]{1,2,0:T(8,128)}, u32[]{:S(2)}, u32[]{:S(2)}) collective-permute-start(f32[2,640,640]{1,2,0:T(8,128)S(1)} %broadcast_multiply_fusion), channel_id=1, source_target_pairs={{1,16},{2,17},{3,18},{4,19},{5,20},{6,21},{7,22},{8,23},{9,24},{10... | collective-permute-start | bytes 9830408 | tf_op jit(solution)/shard_map/ppermute | solution.py:17
  23.6 150.1 %all-gather.5.cloned.1.call-done = f32[2,640,640]{2,1,0:T(8,128)} async-done(((f32[2,40,640]{2,1,0:T(8,128)}), f32[2,640,640]{2,1,0:T(8,128)}) %all-gather.5.cloned.1.call-update) | async-done | bytes 3276816 | tf_op jit(solution)/shard_map/all_gather | solution.py:29
  173.7 7.4 %fusion.4 = f32[2,640,640]{1,2,0:T(8,128)} fusion(f32[2,640,640]{1,2,0:T(8,128)S(1)} %broadcast_multiply_fusion, f32[2,640,640]{2,1,0:T(8,128)} %all-gather.5.cloned.1.call-done), kind=kOutput, calls=%fused_computation.12 | convolution fusion | flops 3145728000 | bytes 8192000 | tf_op jit(solution)/shard_map/rbc,cd->rbd/dot_general | solution.py:31
  181.1 83.2 %all-gather.3.cloned.1.call-done = f32[2,640,640]{2,1,0:T(8,128)} async-done(((f32[2,40,640]{2,1,0:T(8,128)}), f32[2,640,640]{2,1,0:T(8,128)}) %all-gather.3.cloned.1.call-update) | async-done | bytes 3276816 | tf_op jit(solution)/shard_map/all_gather | solution.py:28
  264.3 7.3 %convolution_bitcast_fusion = f32[2,640,640]{1,2,0:T(8,128)S(1)} fusion(f32[2,640,640]{1,2,0:T(8,128)} %fusion.4, f32[2,640,640]{2,1,0:T(8,128)} %all-gather.3.cloned.1.call-done), kind=kOutput, calls=%fused_computation.4 | convolution fusion | flops 3145728000 | bytes 8192000 | tf_op jit(solution)/shard_map/ba,rbd->rad/dot_general | solution.py:32
  271.6 2.4 collective-permute-start.1
  274.0 4.5 %fusion.2 = f32[2,640,640]{1,2,0:T(8,128)S(1)} fusion(f32[2,640,640]{1,2,0:T(8,128)S(1)} %broadcast_multiply_fusion, f32[2,640,640]{2,1,0:T(8,128)S(1)} %copy-done.3), kind=kOutput, calls=%fused_computation.8 | convolution fusion | flops 3145728000 | bytes 8192000 | tf_op jit(solution)/shard_map/rbc,dc->rbd/dot_general | solution.py:35
  278.5 4.8 %fusion.3 = f32[2,640,640]{2,1,0:T(8,128)S(1)} fusion(f32[2,640,640]{1,2,0:T(8,128)S(1)} %broadcast_multiply_fusion, f32[2,640,640]{2,1,0:T(8,128)S(1)} %copy-done.2), kind=kOutput, calls=%fused_computation.10 | convolution fusion | flops 3145728000 | bytes 8192000 | tf_op jit(solution)/shard_map/ab,rbc->rac/dot_general | solution.py:34
  283.3 0.0 collective-permute-done
  283.3 6.8 %fusion.5 = f32[2,640,640]{1,2,0:T(8,128)S(1)} fusion(f32[2,640,640]{1,2,0:T(8,128)} %collective-permute-done, f32[2,640,640]{2,1,0:T(8,128)S(1)} %copy-done.3), kind=kOutput, calls=%fused_computation.13 | convolution fusion | flops 3145728000 | bytes 8192000 | tf_op jit(solution)/shard_map/rbc,dc->rbd/dot_general | solution.py:36
  290.1 105.5 %collective-permute-done.1 = f32[2,640,640]{1,2,0:T(8,128)S(1)} collective-permute-done((f32[2,640,640]{1,2,0:T(8,128)S(1)}, f32[2,640,640]{1,2,0:T(8,128)S(1)}, u32[]{:S(2)}, u32[]{:S(2)}) %collective-permute-start.1) | collective-permute-done | bytes 3276832 | tf_op jit(solution)/shard_map/ppermute | solution.py:17
  395.6 5.2 %fusion.1 = f32[2,640,640]{1,2,0:T(8,128)S(1)} fusion(f32[2,640,640]{1,2,0:T(8,128)S(1)} %collective-permute-done.1, f32[2,640,640]{1,2,0:T(8,128)S(1)} %fusion.2, f32[2,640,640]{2,1,0:T(8,128)S(1)} %fusion.3, f32[2,640,640]{1,2,0:T(8,128)S(1)} %fusion.5, f32[640,640]{0,1:T(8,128)S(1)} %copy-done.1, f32[2,640,640]{2,1,0:T(8,128)S(1)} %copy-done.2), kind=kOutput, calls=%fused_computation.2 | convolution fusion | flops 3149004800 | bytes 19660800 | tf_op jit(solution)/shard_map/ab,rbd->rad/dot_general | solution.py:37
  400.8 3.0 copy.11
  (7 shorter events, 0.0 us)
Async XLA Ops:
  6.5 167.2 %all-gather.5.cloned.1.call-start = ((), (), s32[]{:S(2)}) async-start(), calls=%async_computation.1 | async-start | bytes 3481600 | tf_op jit(solution)/shard_map/all_gather | solution.py:29
  8.2 256.1 %all-gather.3.cloned.1.call-start = ((), (), s32[]{:S(2)}) async-start(), calls=%async_computation | async-start | bytes 3481600 | tf_op jit(solution)/shard_map/all_gather | solution.py:28
  16.0 2.8 copy-start
  18.8 264.5 %collective-permute-start = (f32[2,640,640]{1,2,0:T(8,128)S(1)}, f32[2,640,640]{1,2,0:T(8,128)}, u32[]{:S(2)}, u32[]{:S(2)}) collective-permute-start(f32[2,640,640]{1,2,0:T(8,128)S(1)} %broadcast_multiply_fusion), channel_id=1, source_target_pairs={{1,16},{2,17},{3,18},{4,19},{5,20},{6,21},{7,22},{8,23},{9,24},{10... | collective-permute-start | bytes 9830408 | tf_op jit(solution)/shard_map/ppermute | solution.py:17
  264.3 9.7 %copy-start.3 = (f32[2,640,640]{2,1,0:T(8,128)S(1)}, f32[2,640,640]{2,1,0:T(8,128)}, u32[]{:S(2)}) copy-start(f32[2,640,640]{2,1,0:T(8,128)} %all-gather.5.cloned.1.call-done) | copy-start | bytes 9830404
  271.6 6.9 %copy-start.2 = (f32[2,640,640]{2,1,0:T(8,128)S(1)}, f32[2,640,640]{2,1,0:T(8,128)}, u32[]{:S(2)}) copy-start(f32[2,640,640]{2,1,0:T(8,128)} %all-gather.3.cloned.1.call-done) | copy-start | bytes 9830404
  271.6 124.0 %collective-permute-start.1 = (f32[2,640,640]{1,2,0:T(8,128)S(1)}, f32[2,640,640]{1,2,0:T(8,128)S(1)}, u32[]{:S(2)}, u32[]{:S(2)}) collective-permute-start(f32[2,640,640]{1,2,0:T(8,128)S(1)} %convolution_bitcast_fusion), channel_id=1, source_target_pairs={{16,1},{17,2},{18,3},{19,4},{20,5},{21,6},{22,7},{23,8},{24,9},{25... | collective-permute-start | bytes 9830408 | tf_op jit(solution)/shard_map/ppermute | solution.py:17
  283.3 112.3 %copy-start.1 = (f32[640,640]{0,1:T(8,128)S(1)}, f32[640,640]{0,1:T(8,128)}, u32[]{:S(2)}) copy-start(f32[640,640]{0,1:T(8,128)} %copy-done) | copy-start | bytes 4915204
Sparse Core Ops, SparseCore 0:
  9.1 164.5 all-gather.4
  176.4 87.7 all-gather.2
where the time goes:
time: 411 us
  waiting for transfers between devices  339 us (82%)
  matrix products  35.9 us (9%)
  between operations  14.8 us (4%)
  local copies, waits for them, and re-layouts  7.54 us (2%)
  starting transfers between devices  7.2 us (2%)
  other arithmetic  6.25 us (2%)
    all_gather x1, waiting for transfers between devices, on_device(): lax.all_gather(jnp.concatenate([right_env, right_op]), 'lsec', axis=1, ti...  150 us
    ppermute x2, waiting for transfers between devices, shifted(): return lax.ppermute(value, ('lsec', 'rsec'), pairs)  106 us
    all_gather x1, waiting for transfers between devices, on_device(): lax.all_gather(jnp.concatenate([left_env, left_op]), 'rsec', axis=1, tile...  83.2 us
  transfers between devices with their start and end apart: 4, of which 3 were waited for; matrix products, arithmetic and copies ran while one was open for 10% of the time, Pallas kernels for 0%

commit v1 on v0

--- a/solution.py
+++ b/solution.py
@@ -4,6 +4,13 @@
 from jax.sharding import PartitionSpec as P
 
 HI = lax.Precision.HIGH
+
+
+def match_stops_all(w_in):
+    value_now = jnp.stack([w_in] * lax.axis_size("lsec"), axis=0)
+    long_array = lax.all_to_all(value_now, "lsec", 0, 0)
+    out_arr = jnp.concatenate(long_array, axis=1)
+    return out_arr
 
 
 def shifted(value, step):
@@ -26,7 +33,7 @@
     masked = states * mask[None]
     moved = shifted(masked, 1)
     left = lax.all_gather(jnp.concatenate([left_env, left_op]), "rsec", axis=1, tiled=True)
-    right = lax.all_gather(jnp.concatenate([right_env, right_op]), "lsec", axis=1, tiled=True)
+    right = match_stops_all(jnp.concatenate([right_env, right_op]))
     env_l, oper_l, env_r, oper_r = (left[0], left[1], right[0], right[1])
     right_part = jnp.einsum("rbc,cd->rbd", masked, oper_r, precision=HI)
     source = jnp.einsum("ba,rbd->rad", oper_l, right_part, precision=HI)

time: 411 us -> 324 us (0.79)
  the two profiles are of different devices: /device:TPU:198 before, /device:TPU:251 now
where the time goes in v1:
time: 324 us; the launch traced here: 323 us
  waiting for transfers between devices  242 us (75%)
  matrix products  34.6 us (11%)
  between operations  14.9 us (5%)
  starting transfers between devices  14.7 us (5%)
  local copies, waits for them, and re-layouts  12.4 us (4%)
  other arithmetic  4.63 us (1%)
    ppermute x2, waiting for transfers between devices, shifted(): return lax.ppermute(value, ('lsec', 'rsec'), pairs)  125 us
    all_to_all x1, waiting for transfers between devices, match_stops_all(): long_array = lax.all_to_all(value_now, 'lsec', 0, 0)  62.5 us
    all_gather x1, waiting for transfers between devices, on_device(): lax.all_gather(jnp.concatenate([left_env, left_op]), 'rsec', axis=1, tile...  54.7 us
    ppermute x2, starting transfers between devices, shifted(): return lax.ppermute(value, ('lsec', 'rsec'), pairs)  7.46 us
    dot_general x1, matrix products, on_device(): source = jnp.einsum('ba,rbd->rad', oper_l, right_part, precision=HI)  7.27 us
    all_to_all x1, starting transfers between devices, match_stops_all(): long_array = lax.all_to_all(value_now, 'lsec', 0, 0)  7.25 us
    dot_general x1, matrix products, on_device(): inner = jnp.einsum('rbc,dc->rbd', moved, oper_r, precision=HI)  6.77 us
  transfers between devices with their start and end apart: 4, of which 3 were waited for; matrix products, arithmetic and copies ran while one was open for 12% of the time, Pallas kernels for 0%

profile of v1, /device:TPU:251, one launch (start us, length us, event | category | flops | bytes accessed | tf_op | source)
XLA Modules:
  0.0 323.3 jit_solution(251479620871344336)
XLA Ops:
  6.5 1.0 pad_maximum_fusion.1
  7.5 1.9 stack.2
  9.4 7.2 %all-to-all-start = ((f32[16,2,40,640]{3,2,1,0:T(8,128)}), f32[16,2,40,640]{3,2,1,0:T(8,128)}, u32[]{:S(2)}, u32[]{:S(2)}) async-start(f32[16,2,40,640]{3,2,1,0:T(8,128)} %stack.2), calls=%async_computation | async-start | bytes 6553600 | tf_op jit(solution)/shard_map/all_to_all | solution.py:11
  16.7 0.0 all-gather.2.cloned.1.call-start
  16.8 0.7 pad_maximum_fusion
  17.5 0.0 all-gather.2.cloned.1.call-update
  18.8 3.0 copy.12
  21.8 0.2 broadcast_multiply_fusion.1
  21.9 2.8 broadcast_multiply_fusion
  24.8 6.0 %collective-permute-start = (f32[2,640,640]{1,2,0:T(8,128)S(1)}, f32[2,640,640]{1,2,0:T(8,128)}, u32[]{:S(2)}, u32[]{:S(2)}) collective-permute-start(f32[2,640,640]{1,2,0:T(8,128)S(1)} %broadcast_multiply_fusion), channel_id=1, source_target_pairs={{1,16},{2,17},{3,18},{4,19},{5,20},{6,21},{7,22},{8,23},{9,24},{10... | collective-permute-start | bytes 9830408 | tf_op jit(solution)/shard_map/ppermute | solution.py:24
  30.7 62.5 %all-to-all-done = f32[16,2,40,640]{3,2,1,0:T(8,128)} async-done(((f32[16,2,40,640]{3,2,1,0:T(8,128)}), f32[16,2,40,640]{3,2,1,0:T(8,128)}, u32[]{:S(2)}, u32[]{:S(2)}) %all-to-all-start) | async-done | bytes 3276832 | tf_op jit(solution)/shard_map/all_to_all | solution.py:11
  93.2 3.3 %fusion.5 = (f32[1,16,40,640]{3,2,0,1:T(8,128)}, f32[1,16,40,640]{3,2,0,1:T(8,128)S(1)}) fusion(f32[2,16,40,640]{3,2,0,1:T(8,128)} %bitcast.5), kind=kLoop, calls=%fused_computation.16 | loop fusion | bytes 6553600 | tf_op jit(solution)/shard_map/slice | solution.py:37
  96.6 1.2 copy-done.2
  97.8 6.0 %fusion.8 = f32[2,640,640]{1,2,0:T(8,128)} fusion(f32[2,640,640]{1,2,0:T(8,128)S(1)} %broadcast_multiply_fusion, f32[640,640,1]{1,0,2:T(8,128)S(1)} %bitcast.41), kind=kOutput, calls=%fused_computation.19 | convolution fusion | flops 3145728000 | bytes 8192000 | tf_op jit(solution)/shard_map/rbc,cd->rbd/dot_general | solution.py:38
  103.8 54.7 %all-gather.2.cloned.1.call-done = f32[2,640,640]{2,1,0:T(8,128)} async-done(((f32[2,40,640]{2,1,0:T(8,128)}), f32[2,640,640]{2,1,0:T(8,128)}) %all-gather.2.cloned.1.call-update) | async-done | bytes 3276816 | tf_op jit(solution)/shard_map/all_gather | solution.py:35
  158.5 7.3 %convolution_bitcast_fusion = f32[2,640,640]{1,2,0:T(8,128)S(1)} fusion(f32[2,640,640]{1,2,0:T(8,128)} %fusion.8, f32[2,640,640]{2,1,0:T(8,128)} %all-gather.2.cloned.1.call-done), kind=kOutput, calls=%fused_computation.4 | convolution fusion | flops 3145728000 | bytes 8192000 | tf_op jit(solution)/shard_map/ba,rbd->rad/dot_general | solution.py:39
  165.8 1.5 collective-permute-start.1
  167.3 4.5 %fusion.6 = f32[2,640,640]{1,2,0:T(8,128)S(1)} fusion(f32[2,640,640]{1,2,0:T(8,128)S(1)} %broadcast_multiply_fusion, f32[640,640,1]{1,0,2:T(8,128)S(1)} %bitcast.43), kind=kOutput, calls=%fused_computation.17 | convolution fusion | flops 3145728000 | bytes 8192000 | tf_op jit(solution)/shard_map/rbc,dc->rbd/dot_general | solution.py:42
  171.8 4.8 %fusion.2 = f32[2,640,640]{2,1,0:T(8,128)S(1)} fusion(f32[2,640,640]{1,2,0:T(8,128)S(1)} %broadcast_multiply_fusion, f32[2,640,640]{2,1,0:T(8,128)S(1)} %copy-done.4), kind=kOutput, calls=%fused_computation.7 | convolution fusion | flops 3145728000 | bytes 8192000 | tf_op jit(solution)/shard_map/ab,rbc->rac/dot_general | solution.py:41
  176.6 0.0 collective-permute-done
  176.7 6.8 %fusion.7 = f32[2,640,640]{1,2,0:T(8,128)S(1)} fusion(f32[2,640,640]{1,2,0:T(8,128)} %collective-permute-done, f32[640,640,1]{1,0,2:T(8,128)S(1)} %bitcast.42), kind=kOutput, calls=%fused_computation.18 | convolution fusion | flops 3145728000 | bytes 8192000 | tf_op jit(solution)/shard_map/rbc,dc->rbd/dot_general | solution.py:43
  183.4 124.8 %collective-permute-done.1 = f32[2,640,640]{1,2,0:T(8,128)S(1)} collective-permute-done((f32[2,640,640]{1,2,0:T(8,128)S(1)}, f32[2,640,640]{1,2,0:T(8,128)S(1)}, u32[]{:S(2)}, u32[]{:S(2)}) %collective-permute-start.1) | collective-permute-done | bytes 3276832 | tf_op jit(solution)/shard_map/ppermute | solution.py:24
  308.3 5.2 %fusion.1 = f32[2,640,640]{1,2,0:T(8,128)S(1)} fusion(f32[2,640,640]{1,2,0:T(8,128)S(1)} %collective-permute-done.1, f32[2,640,640]{1,2,0:T(8,128)S(1)} %fusion.6, f32[2,640,640]{2,1,0:T(8,128)S(1)} %fusion.2, f32[2,640,640]{1,2,0:T(8,128)S(1)} %fusion.7, f32[640,640]{0,1:T(8,128)S(1)} %copy-done.1, f32[2,640,640]{2,1,0:T(8,128)S(1)} %copy-done.4), kind=kOutput, calls=%fused_computation.2 | convolution fusion | flops 3149004800 | bytes 19660800 | tf_op jit(solution)/shard_map/ab,rbd->rad/dot_general | solution.py:44
  313.5 3.0 copy.15
  (18 shorter events, 0.0 us)
Async XLA Ops:
  9.4 7.3 %copy-start.7 = (f32[1,40,640]{2,1,0:T(8,128)S(1)}, f32[1,40,640]{2,1,0:T(8,128)}, u32[]{:S(2)}) copy-start(f32[1,40,640]{2,1,0:T(8,128)} %param.10) | copy-start | bytes 307204
  9.4 7.3 %copy-start.8 = (f32[1,40,640]{2,1,0:T(8,128)S(1)}, f32[1,40,640]{2,1,0:T(8,128)}, u32[]{:S(2)}) copy-start(f32[1,40,640]{2,1,0:T(8,128)} %param.8) | copy-start | bytes 307204
  9.4 9.3 %copy-start.6 = (f32[2,640,640]{2,1,0:T(8,128)S(1)}, f32[2,640,640]{2,1,0:T(8,128)}, u32[]{:S(2)}) copy-start(f32[2,640,640]{2,1,0:T(8,128)} %param.7) | copy-start | bytes 9830404
  9.4 83.8 %all-to-all-start = ((f32[16,2,40,640]{3,2,1,0:T(8,128)}), f32[16,2,40,640]{3,2,1,0:T(8,128)}, u32[]{:S(2)}, u32[]{:S(2)}) async-start(f32[16,2,40,640]{3,2,1,0:T(8,128)} %stack.2), calls=%async_computation | async-start | bytes 6553600 | tf_op jit(solution)/shard_map/all_to_all | solution.py:11
  16.7 141.8 %all-gather.2.cloned.1.call-start = ((), (), s32[]{:S(2)}) async-start(), calls=%async_computation.1 | async-start | bytes 3481600 | tf_op jit(solution)/shard_map/all_gather | solution.py:35
  21.9 2.8 copy-start
  24.8 151.9 %collective-permute-start = (f32[2,640,640]{1,2,0:T(8,128)S(1)}, f32[2,640,640]{1,2,0:T(8,128)}, u32[]{:S(2)}, u32[]{:S(2)}) collective-permute-start(f32[2,640,640]{1,2,0:T(8,128)S(1)} %broadcast_multiply_fusion), channel_id=1, source_target_pairs={{1,16},{2,17},{3,18},{4,19},{5,20},{6,21},{7,22},{8,23},{9,24},{10... | collective-permute-start | bytes 9830408 | tf_op jit(solution)/shard_map/ppermute | solution.py:24
  96.6 1.2 copy-start.2
  158.5 8.8 %copy-start.5 = (f32[1,16,40,640]{3,2,0,1:T(8,128)S(1)}, f32[1,16,40,640]{3,2,0,1:T(8,128)}, u32[]{:S(2)}) copy-start(f32[1,16,40,640]{3,2,0,1:T(8,128)} %get-tuple-element.5) | copy-start | bytes 4915204
  165.8 142.5 %collective-permute-start.1 = (f32[2,640,640]{1,2,0:T(8,128)S(1)}, f32[2,640,640]{1,2,0:T(8,128)S(1)}, u32[]{:S(2)}, u32[]{:S(2)}) collective-permute-start(f32[2,640,640]{1,2,0:T(8,128)S(1)} %convolution_bitcast_fusion), channel_id=1, source_target_pairs={{16,1},{17,2},{18,3},{19,4},{20,5},{21,6},{22,7},{23,8},{24,9},{25... | collective-permute-start | bytes 9830408 | tf_op jit(solution)/shard_map/ppermute | solution.py:24
  167.3 4.5 %copy-start.4 = (f32[2,640,640]{2,1,0:T(8,128)S(1)}, f32[2,640,640]{2,1,0:T(8,128)}, u32[]{:S(2)}) copy-start(f32[2,640,640]{2,1,0:T(8,128)} %all-gather.2.cloned.1.call-done) | copy-start | bytes 9830404
  171.8 4.9 %copy-start.3 = (f32[1,16,40,640]{3,2,0,1:T(8,128)S(1)}, f32[1,16,40,640]{3,2,0,1:T(8,128)}, u32[]{:S(2)}) copy-start(f32[1,16,40,640]{3,2,0,1:T(8,128)} %copy-done.2) | copy-start | bytes 4915204
  176.6 131.6 %copy-start.1 = (f32[640,640]{0,1:T(8,128)S(1)}, f32[640,640]{0,1:T(8,128)}, u32[]{:S(2)}) copy-start(f32[640,640]{0,1:T(8,128)} %copy-done) | copy-start | bytes 4915204
Sparse Core Ops, SparseCore 0:
  20.3 138.1 all-gather.1
